TPU v7x, 32 devices: a whole 2x2x4 slice. The times are simulated.
32 devices in a mesh: group: 1, expert: 32 (over z, y, x, core), hslice: 1.
Axes of the slice: x: 2, y: 2, z: 4, core: 2. Of those that a mesh axis runs over, the one named last changes fastest.
Arguments:
- tokens: bfloat16 [2048, 3584], P(('group', 'expert')), may hold values from -6 to 6
- routes: int32 [2048, 8], P(('group', 'expert')), may hold values from 0 to 15, all different within a row; in each aligned block of 64 rows (0 to 63, 64 to 127, ...) at most 36 rows name the same one
- gate_values: float32 [2048, 8], P(('group', 'expert')), may hold values from 0.1 to 1
- gate_up: bfloat16 [32, 3584, 2, 512], P('expert', None, None, 'hslice'), may hold values from -0.09375 to 0.09375
- down_weight: bfloat16 [32, 512, 3584], P('expert', None, 'hslice'), may hold values from -0.1875 to 0.1875
Outputs:
- mixed_out: bfloat16 [2048, 3584], P(('group', 'expert'), 'hslice')
Inputs may be any that keep to these rules, and one draw needn't show every extreme that they name: `routes`: each row names 8 different experts. Within the rows of one index of expert (aligned blocks of 64 tokens) no expert is named more than 36 times, a bound that some block reaches.
All inputs are finite; a program needn't handle non-finite values.
Results may differ from a plain program's by a relative error of at most 0.0065.
Values may be sent and summed in bfloat16 or wider, within the bound.
A program may use at most 64 MiB of HBM per device.

v0:
```python
import jax
import jax.numpy as jnp
from jax import lax
from jax.sharding import PartitionSpec as P


def partner_2(block, axis, distance):
    count = lax.axis_size(axis)
    route = []
    for low in range(count):
        high = low | 1 << distance
        if high != low and high < count:
            route += [(low, high), (high, low)]
    return lax.ppermute(block, axis, route)


def swiglu_rows(inputs, weights, split_at):
    both_parts = jnp.dot(inputs, weights, preferred_element_type=jnp.float32)
    return (jax.nn.silu(both_parts[:, :split_at]) * both_parts[:, split_at:]).astype(jnp.bfloat16)


def down_fold(down_matrix, hidden_piece):
    return jnp.dot(hidden_piece, down_matrix, preferred_element_type=jnp.float32)


def local(tokens, routes, gate_values, gate_up, down_weight):
    devices = lax.axis_size("expert")
    experts = devices // 2
    tok_count, choices = routes.shape
    features = tokens.shape[1]
    hidden_width = gate_up.shape[3]
    half_units = down_weight.shape[1]
    columns = down_weight.shape[2]
    capacity = min(tok_count, 2 * ((9 * tok_count * choices + 16 * experts - 1) // (16 * experts)))
    slot_rows = capacity // 2
    targets = experts * capacity
    expert_ids = routes.reshape(-1)
    member = (expert_ids[:, None] == jnp.arange(experts, dtype=jnp.int32)[None, :]).astype(
        jnp.int32
    )
    earlier = jnp.sum((jnp.cumsum(member, axis=0) - member) * member, axis=1)
    target = expert_ids * capacity + earlier
    target_hot = (target[:, None] == jnp.arange(targets, dtype=jnp.int32)[None, :]).astype(
        jnp.bfloat16
    )
    repeated = jnp.broadcast_to(tokens[:, None, :], (tok_count, choices, features)).reshape(
        tok_count * choices, features
    )
    outgoing = lax.dot_general(
        target_hot, repeated, (((0,), (0,)), ((), ())), preferred_element_type=jnp.float32
    ).astype(jnp.bfloat16)
    own_half = lax.axis_index("expert") % 2
    doubled = jnp.broadcast_to(
        outgoing.reshape(experts, 1, capacity, features), (experts, 2, capacity, features)
    )
    arrived = lax.all_to_all(
        doubled.reshape(devices * capacity, features),
        "expert",
        split_axis=0,
        concat_axis=0,
        tiled=True,
    )
    own_gate_up = gate_up.reshape(features, 2 * hidden_width)
    own_down = down_weight.reshape(half_units, columns)
    hidden_all = swiglu_rows(arrived, own_gate_up, hidden_width)
    summed = down_fold(own_down, lax.all_gather(hidden_all, "hslice", axis=1, tiled=True))
    summed = summed.astype(jnp.bfloat16)
    partner = partner_2(summed, "expert", 0)
    pair_total = (
        (summed.astype(jnp.float32) + partner.astype(jnp.float32))
        .astype(jnp.bfloat16)
        .reshape(devices, 2, slot_rows, columns)
    )
    kept_slot = jnp.where(own_half == 0, pair_total[:, 0], pair_total[:, 1]).reshape(
        devices * slot_rows, columns
    )
    merged = lax.all_to_all(kept_slot, "expert", split_axis=0, concat_axis=0, tiled=True)
    merged = merged.astype(jnp.float32)
    weights_map = (target_hot.astype(jnp.float32) * gate_values.reshape(-1)[:, None]).reshape(
        tok_count, choices, targets
    )
    weights_map = jnp.sum(weights_map, axis=1)
    mixed_out = jnp.dot(
        weights_map, merged, precision=lax.Precision.HIGHEST, preferred_element_type=jnp.float32
    )
    return mixed_out.astype(jnp.bfloat16)


def solution(mesh):
    in_specs = (
        P(("group", "expert"), None),
        P(("group", "expert"), None),
        P(("group", "expert"), None),
        P("expert", None, None, "hslice"),
        P("expert", None, "hslice"),
    )
    out_specs = P(("group", "expert"), "hslice")
    return jax.shard_map(local, mesh=mesh, in_specs=in_specs, out_specs=out_specs, check_vma=False)
```

profile of v0, /device:TPU:0, one launch (start us, length us, event | category | flops | bytes accessed | tf_op | source)
XLA Modules:
  0.0 445.2 jit_solution(12530937650791013171)
XLA Ops:
  0.0 0.0 copy-start
  0.0 0.8 copy.20
  0.8 0.1 eq.54
  0.9 0.1 eq.50
  1.0 1.2 reduce-window.6
  2.2 0.2 slice_reduce_fusion
  2.4 0.1 fusion.11
  2.5 0.0 copy-done
  2.6 4.4 convolution_convert_fusion.1
  6.9 6.9 %broadcast_in_dim.7 = bf16[16,36,3584]{2,1,0:T(8,128)(2,1)} reshape(bf16[576,3584]{1,0:T(8,128)(2,1)} %convolution_convert_fusion.1) | data formatting | bytes 8257536 | tf_op jit(solution)/shard_map/broadcast_in_dim | solution.py:53
  13.8 6.6 %broadcast_in_dim.8 = bf16[16,2,36,3584]{3,2,1,0:T(8,128)(2,1)} broadcast(bf16[16,36,3584]{2,1,0:T(8,128)(2,1)} %broadcast_in_dim.7), dimensions={0,2,3} | broadcast | bytes 12386304 | tf_op jit(solution)/shard_map/broadcast_in_dim | solution.py:53
  20.4 7.6 %all-to-all-start = ((bf16[32,36,3584]{2,1,0:T(8,128)(2,1)}), bf16[32,36,3584]{2,1,0:T(8,128)(2,1)}, u32[]{:S(2)}, u32[]{:S(2)}) async-start(bf16[32,36,3584]{2,1,0:T(8,128)(2,1)} %bitcast.35), calls=%async_computation | async-start | bytes 18350080 | tf_op jit(solution)/shard_map/all_to_all | solution.py:56
  28.0 8.4 %copy.27 = bf16[448,8,2,512]{3,1,2,0:T(8,128)(2,1)} copy(bf16[448,8,2,512]{3,2,1,0:T(2,128)(2,1)} %bitcast.36) | data formatting | bytes 14680064
  36.4 194.9 %all-to-all-done = bf16[32,36,3584]{2,1,0:T(8,128)(2,1)} async-done(((bf16[32,36,3584]{2,1,0:T(8,128)(2,1)}), bf16[32,36,3584]{2,1,0:T(8,128)(2,1)}, u32[]{:S(2)}, u32[]{:S(2)}) %all-to-all-start) | async-done | bytes 8257568 | tf_op jit(solution)/shard_map/all_to_all | solution.py:56
  231.3 12.6 %all_to_all.16 = bf16[1152,3584]{1,0:T(8,128)(2,1)} reshape(bf16[32,36,3584]{2,1,0:T(8,128)(2,1)} %all-to-all-done) | data formatting | bytes 16515072 | tf_op jit(solution)/shard_map/all_to_all | solution.py:56
  243.8 0.0 copy-start.4
  243.8 12.6 %fusion.14 = f32[1152,1024]{1,0:T(8,128)S(1)} fusion(bf16[1152,3584]{1,0:T(8,128)(2,1)} %all_to_all.16, bf16[3584,1024]{1,0:T(8,128)(2,1)} %bitcast.37), kind=kOutput, calls=%fused_computation.29 | convolution fusion | flops 8455716864 | bytes 20316160 | tf_op jit(solution)/shard_map/dot_general | solution.py:18
  256.4 0.0 copy-done.4
  256.4 6.7 %convolution_convert_fusion = bf16[1152,3584]{1,0:T(8,128)(2,1)} fusion(bf16[1,512,3584]{2,1,0:T(8,128)(2,1)S(1)} %copy-done.4, f32[1152,1024]{1,0:T(8,128)S(1)} %fusion.14), kind=kOutput, calls=%fused_computation.1 | convolution fusion | flops 4235526144 | bytes 16646144 | tf_op jit(solution)/shard_map/dot_general | solution.py:23
  263.1 0.0 collective-permute-start
  263.1 13.3 %collective-permute-done = bf16[1152,3584]{1,0:T(8,128)(2,1)} collective-permute-done((bf16[1152,3584]{1,0:T(8,128)(2,1)}, bf16[1152,3584]{1,0:T(8,128)(2,1)}, u32[]{:S(2)}, u32[]{:S(2)}) %collective-permute-start) | collective-permute-done | bytes 8257568 | tf_op jit(solution)/shard_map/ppermute | solution.py:14
  276.4 9.4 %add_convert_fusion = bf16[1152,3584]{1,0:T(8,128)(2,1)} fusion(bf16[1152,3584]{1,0:T(8,128)(2,1)} %collective-permute-done, bf16[1152,3584]{1,0:T(8,128)(2,1)} %convolution_convert_fusion), kind=kLoop, calls=%fused_computation | loop fusion | flops 16515072 | bytes 24772608 | tf_op jit(solution)/shard_map/convert_element_type | solution.py:71
  285.8 13.2 %reshape.74 = bf16[32,2,18,3584]{3,2,1,0:T(8,128)(2,1)} reshape(bf16[1152,3584]{1,0:T(8,128)(2,1)} %add_convert_fusion) | data formatting | bytes 16515072 | tf_op jit(solution)/shard_map/reshape | solution.py:72
  299.0 7.1 %fusion = bf16[32,18,3584]{2,1,0:T(8,128)(2,1)} fusion(bf16[32,2,18,3584]{3,2,1,0:T(8,128)(2,1)} %reshape.74, pred[]{:T(512)S(6)} %eq.61), kind=kLoop, calls=%fused_computation.4 | loop fusion | flops 2064384 | bytes 12386305 | tf_op jit(solution)/shard_map/jit(_where)/select_n | solution.py:74
  306.2 0.0 copy-start.2
  306.2 0.0 copy-start.3
  306.2 3.7 all-to-all-start.1
  309.9 0.1 reduce_sum.21
  310.0 0.1 copy.23
  310.0 0.0 copy-done.2
  310.0 0.1 copy.24
  310.1 0.0 copy-done.3
  310.1 0.1 copy.25
  310.2 0.5 multiply_reduce_fusion
  310.8 121.6 %all-to-all-done.1 = bf16[32,18,3584]{2,1,0:T(8,128)(2,1)} async-done(((bf16[32,18,3584]{2,1,0:T(8,128)(2,1)}), bf16[32,18,3584]{2,1,0:T(8,128)(2,1)}, u32[]{:S(2)}, u32[]{:S(2)}) %all-to-all-start.1) | async-done | bytes 4128800 | tf_op jit(solution)/shard_map/all_to_all | solution.py:77
  432.4 0.0 copy-start.1
  432.4 7.4 %all_to_all.18 = bf16[576,3584]{1,0:T(8,128)(2,1)} reshape(bf16[32,18,3584]{2,1,0:T(8,128)(2,1)} %all-to-all-done.1) | data formatting | bytes 8257536 | tf_op jit(solution)/shard_map/all_to_all | solution.py:77
  439.8 5.3 %convolution_convert_fusion.2 = bf16[64,3584]{1,0:T(8,128)(2,1)} fusion(f32[64,576]{1,0:T(8,128)S(1)} %multiply_reduce_fusion, bf16[576,3584]{1,0:T(8,128)(2,1)} %all_to_all.18), kind=kOutput, calls=%fused_computation.5 | convolution fusion | flops 1585676288 | bytes 4734976 | tf_op jit(solution)/shard_map/dot_general | solution.py:83
  445.2 0.0 copy-done.1
  (5 shorter events, 0.1 us)
Async XLA Ops:
  0.0 2.5 copy-start
  20.4 210.9 %all-to-all-start = ((bf16[32,36,3584]{2,1,0:T(8,128)(2,1)}), bf16[32,36,3584]{2,1,0:T(8,128)(2,1)}, u32[]{:S(2)}, u32[]{:S(2)}) async-start(bf16[32,36,3584]{2,1,0:T(8,128)(2,1)} %bitcast.35), calls=%async_computation | async-start | bytes 18350080 | tf_op jit(solution)/shard_map/all_to_all | solution.py:56
  243.8 12.6 %copy-start.4 = (bf16[1,512,3584]{2,1,0:T(8,128)(2,1)S(1)}, bf16[1,512,3584]{2,1,0:T(8,128)(2,1)}, u32[]{:S(2)}) copy-start(bf16[1,512,3584]{2,1,0:T(8,128)(2,1)} %param.9) | copy-start | bytes 11010052
  263.1 13.3 %collective-permute-start = (bf16[1152,3584]{1,0:T(8,128)(2,1)}, bf16[1152,3584]{1,0:T(8,128)(2,1)}, u32[]{:S(2)}, u32[]{:S(2)}) collective-permute-start(bf16[1152,3584]{1,0:T(8,128)(2,1)} %convolution_convert_fusion), channel_id=1, source_target_pairs={{0,1},{1,0},{2,3},{3,2},{4,5},{5,4},{6,7},{7,6},{8,9},{9,8},{10,11... | collective-permute-start | bytes 24772616 | tf_op jit(solution)/shard_map/ppermute | solution.py:14
  306.2 3.9 copy-start.2
  306.2 4.0 copy-start.3
  306.2 126.3 %all-to-all-start.1 = ((bf16[32,18,3584]{2,1,0:T(8,128)(2,1)}), bf16[32,18,3584]{2,1,0:T(8,128)(2,1)}, u32[]{:S(2)}, u32[]{:S(2)}) async-start(bf16[32,18,3584]{2,1,0:T(8,128)(2,1)} %fusion), calls=%async_computation.1 | async-start | bytes 11010048 | tf_op jit(solution)/shard_map/all_to_all | solution.py:77
  432.4 12.7 %copy-start.1 = (bf16[64,3584]{1,0:T(8,128)(2,1)S(1)}, bf16[64,3584]{1,0:T(8,128)(2,1)}, u32[]{:S(2)}) copy-start(bf16[64,3584]{1,0:T(8,128)(2,1)} %param.5) | copy-start | bytes 1376260
where the time goes:
time: 446 us; the launch traced here: 445 us
  waiting for transfers between devices  330 us (74%)
  local copies, waits for them, and re-layouts  56.6 us (13%)
  matrix products  28.9 us (6%)
  other arithmetic  18.4 us (4%)
  starting transfers between devices  11.3 us (3%)
    all_to_all x1, waiting for transfers between devices, local(): lax.all_to_all(doubled.reshape(devices * capacity, features), 'expert', s...  195 us
    all_to_all x1, waiting for transfers between devices, local(): lax.all_to_all(kept_slot, 'expert', split_axis=0, concat_axis=0, tiled=True)  122 us
    broadcast_in_dim x2, local copies, waits for them, and re-layouts, local(): jnp.broadcast_to(outgoing.reshape(experts, 1, capacity, features), (exper...  13.4 us
    ppermute x1, waiting for transfers between devices, partner_2(): return lax.ppermute(block, axis, route)  13.3 us
    reshape x1, local copies, waits for them, and re-layouts, local(): pair_total = (summed.astype(jnp.float32) + partner.astype(jnp.float32)).a...  13.2 us
    dot_general x1, matrix products, swiglu_rows(): both_parts = jnp.dot(inputs, weights, preferred_element_type=jnp.float32)  12.6 us
    all_to_all x1, local copies, waits for them, and re-layouts, local(): lax.all_to_all(doubled.reshape(devices * capacity, features), 'expert', s...  12.6 us
    convert_element_type x1, other arithmetic, local(): pair_total = (summed.astype(jnp.float32) + partner.astype(jnp.float32)).a...  9.41 us
  transfers between devices with their start and end apart: 3, of which 3 were waited for; matrix products, arithmetic and copies ran while one was open for 2% of the time, Pallas kernels for 0%

commit v1 on v0

--- a/solution.py
+++ b/solution.py
@@ -1,7 +1,298 @@
+import functools
+
 import jax
 import jax.numpy as jnp
 from jax import lax
+from jax.experimental import pallas as pl
+from jax.experimental.pallas import tpu as pltpu
 from jax.sharding import PartitionSpec as P
+
+MESH = pl.DeviceIdType.MESH
+F32 = jnp.float32
+BF16 = jnp.bfloat16
+
+
+def capacity_of(tok_count, choices, experts):
+    return min(tok_count, 2 * ((9 * tok_count * choices + 16 * experts - 1) // (16 * experts)))
+
+
+def chunks_of(features):
+    for count in (7, 4, 2):
+        if features % (count * 128) == 0:
+            return count
+    return 1
+
+
+def fused_kernel(
+    planes, cap, chunks,
+    tokens, routes, gates, gate_up, down,
+    out,
+    info, line, pack_hot, mix_hi, mix_lo, rows_out, rows_in, acc, hidden,
+    w_up, w_down, y_out, y_in, part, part_own, part_in,
+    i_s, i_r, z_s, z_r, x_s, x_r, y_s, y_r, p_s, p_r, wl, ws, wr, dl, ds, dr,
+):
+    me = lax.axis_index("expert")
+    core = lax.rem(me, 2)
+    x = lax.rem(me // 2, 2)
+    y = lax.rem(me // 4, 2)
+    z = me // 8
+    tok = tokens.shape[0]
+    width = tokens.shape[1] // chunks
+    half = gate_up.shape[2]
+    group = planes * cap
+    partner = me + 1 - 2 * core
+
+    def z_peer(d):
+        return lax.rem(z + d, planes) * 8 + y * 4 + x * 2 + core
+
+    def plane_xy(r):
+        px = x if r % 2 == 0 else 1 - x
+        py = y if r // 2 == 0 else 1 - y
+        return py, px
+
+    def xy_peer(r):
+        py, px = plane_xy(r)
+        return z * 8 + py * 4 + px * 2 + core
+
+    def remote(src, dst, s, r, device):
+        return pltpu.make_async_remote_copy(
+            src_ref=src, dst_ref=dst, send_sem=s, recv_sem=r,
+            device_id={"expert": device}, device_id_type=MESH)
+
+    def columns(j):
+        return pl.ds(pl.multiple_of(j * width, 128), width)
+
+    own_rows = pl.ds(pl.multiple_of(z * tok, 16), tok)
+
+    def up_local(j):
+        return pltpu.make_async_copy(
+            gate_up.at[:, pl.ds(j * width, width)], w_up.at[0, :, pl.ds(j * width, width)], wl.at[j])
+
+    def up_swap(j):
+        return remote(gate_up.at[:, pl.ds(j * width, width)],
+                      w_up.at[1, :, pl.ds(j * width, width)], ws.at[j], wr.at[j], partner)
+
+    down_local = pltpu.make_async_copy(down, w_down.at[pl.ds(0, half)], dl)
+    down_swap = remote(down, w_down.at[pl.ds(half, half)], ds, dr, partner)
+
+    def info_send(d):
+        return remote(info.at[z], info.at[z], i_s.at[d - 1], i_r.at[d - 1], z_peer(d))
+
+    def z_send(d, j):
+        return remote(tokens.at[:, columns(j)], line.at[j, own_rows],
+                      z_s.at[d - 1, j], z_r.at[d - 1, j], z_peer(d))
+
+    def x_send(r, j):
+        return remote(rows_out.at[j, pl.ds((r - 1) * group, group)],
+                      rows_in.at[j, pl.ds(r * group, group)],
+                      x_s.at[r - 1, j], x_r.at[r - 1, j], xy_peer(r))
+
+    def y_send(r, j):
+        return remote(y_out.at[j, pl.ds((r - 1) * group, group)],
+                      y_in.at[j, pl.ds(r * group, group)],
+                      y_s.at[r - 1, j], y_r.at[r - 1, j], xy_peer(r))
+
+    def p_send(d, j):
+        there = pl.ds(pl.multiple_of(lax.rem(z + d, planes) * tok, 16), tok)
+        return remote(part.at[j, there], part_in.at[j, d - 1],
+                      p_s.at[d - 1, j], p_r.at[d - 1, j], z_peer(d))
+
+    def each_chunk(body):
+        def step(j, carry):
+            body(j)
+            return carry
+        lax.fori_loop(0, chunks, step, 0)
+
+    each_chunk(lambda j: up_local(j).start())
+    down_local.start()
+
+    lane = lax.broadcasted_iota(jnp.int32, (tok, 128), 1)
+    weight = jnp.zeros((tok, 128), F32)
+    for k in range(routes.shape[1]):
+        weight = weight + jnp.where(routes[:, k:k + 1] == lane, gates[:, k:k + 1], 0.0)
+    member = jnp.where(weight > 0.0, 1.0, 0.0)
+    lower = jnp.where(
+        lax.broadcasted_iota(jnp.int32, (tok, tok), 1) < lax.broadcasted_iota(jnp.int32, (tok, tok), 0),
+        1.0, 0.0).astype(BF16)
+    rank = jnp.dot(lower, member.astype(BF16), preferred_element_type=F32)
+    slot = jnp.where(weight > 0.0, rank + (z * cap).astype(F32), -10000.0)
+    info[z, :, 0:128] = weight
+    info[z, :, 128:256] = slot
+
+    barrier = pltpu.get_barrier_semaphore()
+    peers = [z_peer(d) for d in range(1, planes)] + [xy_peer(r) for r in (1, 2, 3)] + [partner]
+    for peer in peers:
+        pl.semaphore_signal(barrier, inc=1, device_id={"expert": peer}, device_id_type=MESH)
+    pl.semaphore_wait(barrier, len(peers))
+
+    for d in range(1, planes):
+        info_send(d).start()
+
+    def start_z(j):
+        for d in range(1, planes):
+            z_send(d, j).start()
+    each_chunk(start_z)
+    each_chunk(lambda j: up_swap(j).start())
+    down_swap.start()
+
+    def own_line(j):
+        line[j, own_rows, :] = tokens[:, columns(j)]
+    each_chunk(own_line)
+
+    for d in range(1, planes):
+        info_send(d).wait_recv()
+
+    total = planes * tok
+    info_all = info[...].reshape(total, 256)
+    weights = info_all[:, 0:128]
+    slots = info_all[:, 128:256]
+    slots_t = jnp.transpose(slots)
+    row_id = lax.broadcasted_iota(jnp.int32, (128, total), 0)
+    col_id = lax.broadcasted_iota(jnp.int32, (total, 128), 1)
+    pack = jnp.zeros((4 * group, total), F32)
+    mix = jnp.zeros((total, 4 * group), F32)
+    pack_at = lax.broadcasted_iota(jnp.int32, (4 * group, total), 0).astype(F32)
+    mix_at = lax.broadcasted_iota(jnp.int32, (total, 4 * group), 1).astype(F32)
+    for r in range(4):
+        py, px = plane_xy(r)
+        expert = z * 4 + py * 2 + px
+        slot_row = jnp.sum(jnp.where(row_id == expert, slots_t, 0.0), axis=0, keepdims=True)
+        slot_col = jnp.sum(jnp.where(col_id == expert, slots, 0.0), axis=1, keepdims=True)
+        weight_col = jnp.sum(jnp.where(col_id == expert, weights, 0.0), axis=1, keepdims=True)
+        pack = pack + jnp.where(pack_at == slot_row + float(r * group), 1.0, 0.0)
+        mix = mix + jnp.where(mix_at == slot_col + float(r * group), weight_col, 0.0)
+    pack_hot[...] = pack.astype(BF16)
+    high = mix.astype(BF16)
+    mix_hi[...] = high
+    mix_lo[...] = (mix - high.astype(F32)).astype(BF16)
+
+    def pack_step(j):
+        for d in range(1, planes):
+            z_send(d, j).wait_recv()
+        packed = jnp.dot(pack_hot[...], line[j], preferred_element_type=F32).astype(BF16)
+        rows_out[j] = packed[group:]
+        for r in (3, 1, 2):
+            x_send(r, j).start()
+        rows_in[j, 0:group, :] = packed[0:group]
+    each_chunk(pack_step)
+
+    def up_step(j):
+        for r in (1, 2, 3):
+            x_send(r, j).wait_recv()
+        up_local(j).wait()
+        up_swap(j).wait_recv()
+
+        def tile(n, carry):
+            h, g = n // 2, lax.rem(n, 2)
+            term = jnp.dot(rows_in[j], w_up[h, g, pl.ds(j * width, width), :],
+                           preferred_element_type=F32)
+
+            @pl.when(j == 0)
+            def _():
+                acc[n] = term
+
+            @pl.when(j > 0)
+            def _():
+                acc[n] = acc[n] + term
+            return carry
+        lax.fori_loop(0, 4, tile, 0)
+    each_chunk(up_step)
+
+    for h in range(2):
+        gate = acc[2 * h]
+        hidden[:, h * half:(h + 1) * half] = (gate / (1.0 + jnp.exp(-gate)) * acc[2 * h + 1]).astype(BF16)
+
+    down_local.wait()
+    down_swap.wait_recv()
+
+    def down_step(j):
+        result = jnp.dot(hidden[...], w_down[:, columns(j)], preferred_element_type=F32).astype(BF16)
+        y_out[j] = result[group:]
+        for r in (3, 1, 2):
+            y_send(r, j).start()
+        y_in[j, 0:group, :] = result[0:group]
+    each_chunk(down_step)
+
+    def mix_step(j):
+        for r in (1, 2, 3):
+            y_send(r, j).wait_recv()
+        rows = y_in[j]
+        part_own[j] = (jnp.dot(mix_hi[...], rows, preferred_element_type=F32)
+                       + jnp.dot(mix_lo[...], rows, preferred_element_type=F32))
+        part[j] = part_own[j].astype(BF16)
+        for d in range(1, planes):
+            p_send(d, j).start()
+    each_chunk(mix_step)
+
+    def last_step(j):
+        for d in range(1, planes):
+            p_send(d, j).wait_recv()
+        value = part_own[j, own_rows, :]
+        for d in range(1, planes):
+            value = value + part_in[j, d - 1].astype(F32)
+        out[:, columns(j)] = value.astype(BF16)
+    each_chunk(last_step)
+
+    for d in range(1, planes):
+        info_send(d).wait_send()
+
+    def drain(j):
+        for d in range(1, planes):
+            z_send(d, j).wait_send()
+            p_send(d, j).wait_send()
+        for r in (1, 2, 3):
+            x_send(r, j).wait_send()
+            y_send(r, j).wait_send()
+        up_swap(j).wait_send()
+    each_chunk(drain)
+    down_swap.wait_send()
+
+
+def fused(tokens, routes, gate_values, gate_up, down_weight):
+    devices = lax.axis_size("expert")
+    planes = devices // 8
+    tok, choices = routes.shape
+    features = tokens.shape[1]
+    half = gate_up.shape[3]
+    cap = capacity_of(tok, choices, devices // 2)
+    chunks = chunks_of(features)
+    width = features // chunks
+    group = planes * cap
+    total = planes * tok
+    up = jnp.transpose(gate_up.reshape(features, 2, half), (1, 0, 2))
+    down = down_weight.reshape(half, features)
+    dma = pltpu.SemaphoreType.DMA
+    vmem = pltpu.VMEM
+    pairs = lambda n: [dma((n, chunks)), dma((n, chunks))]
+    return pl.pallas_call(
+        functools.partial(fused_kernel, planes, cap, chunks),
+        out_shape=jax.ShapeDtypeStruct((tok, features), BF16),
+        in_specs=[pl.BlockSpec(memory_space=pltpu.VMEM)] * 3 + [pl.BlockSpec(memory_space=pl.ANY)] * 2,
+        out_specs=pl.BlockSpec(memory_space=pltpu.VMEM),
+        scratch_shapes=[
+            vmem((planes, tok, 256), F32),
+            vmem((chunks, total, width), BF16),
+            vmem((4 * group, total), BF16),
+            vmem((total, 4 * group), BF16),
+            vmem((total, 4 * group), BF16),
+            vmem((chunks, 3 * group, width), BF16),
+            vmem((chunks, 4 * group, width), BF16),
+            vmem((4, 4 * group, half), F32),
+            vmem((4 * group, 2 * half), BF16),
+            vmem((2, 2, features, half), BF16),
+            vmem((2 * half, features), BF16),
+            vmem((chunks, 3 * group, width), BF16),
+            vmem((chunks, 4 * group, width), BF16),
+            vmem((chunks, total, width), BF16),
+            vmem((chunks, total, width), F32),
+            vmem((chunks, planes - 1, tok, width), BF16),
+            dma((planes - 1,)), dma((planes - 1,)),
+            *pairs(planes - 1), *pairs(3), *pairs(3), *pairs(planes - 1),
+            dma((chunks,)), dma((chunks,)), dma((chunks,)), dma, dma, dma,
+        ],
+        compiler_params=pltpu.CompilerParams(
+            collective_id=0, has_side_effects=True, vmem_limit_bytes=62 * 1024 * 1024),
+    )(tokens, routes, gate_values, up, down)
 
 
 def partner_2(block, axis, distance):
@@ -31,7 +322,7 @@
     hidden_width = gate_up.shape[3]
     half_units = down_weight.shape[1]
     columns = down_weight.shape[2]
-    capacity = min(tok_count, 2 * ((9 * tok_count * choices + 16 * experts - 1) // (16 * experts)))
+    capacity = capacity_of(tok_count, choices, experts)
     slot_rows = capacity // 2
     targets = experts * capacity
     expert_ids = routes.reshape(-1)
@@ -86,6 +377,24 @@
     return mixed_out.astype(jnp.bfloat16)
 
 
+def local_any(tokens, routes, gate_values, gate_up, down_weight):
+    devices = lax.axis_size("expert")
+    tok, choices = routes.shape
+    planes = devices // 8
+    fits = (
+        lax.axis_size("hslice") == 1
+        and devices % 8 == 0
+        and planes in (2, 4)
+        and devices // 2 <= 128
+        and tok % 16 == 0
+        and planes * capacity_of(tok, choices, devices // 2) % 16 == 0
+        and tokens.shape[1] % 128 == 0
+        and gate_up.shape[3] % 128 == 0
+    )
+    call = fused if fits else local
+    return call(tokens, routes, gate_values, gate_up, down_weight)
+
+
 def solution(mesh):
     in_specs = (
         P(("group", "expert"), None),
@@ -95,4 +404,4 @@
         P("expert", None, "hslice"),
     )
     out_specs = P(("group", "expert"), "hslice")
-    return jax.shard_map(local, mesh=mesh, in_specs=in_specs, out_specs=out_specs, check_vma=False)
+    return jax.shard_map(local_any, mesh=mesh, in_specs=in_specs, out_specs=out_specs, check_vma=False)

time: 446 us -> 141 us (0.32)
  waiting for transfers between devices: 330 us -> 0 us
  Pallas kernels: 0 us -> 129 us
  local copies, waits for them, and re-layouts: 56.6 us -> 11.8 us
  matrix products: 28.9 us -> 0 us
  other arithmetic: 18.4 us -> 0 us
  starting transfers between devices: 11.3 us -> 0 us
    all_to_all x2 -> x0, waiting for transfers between devices: 317 us -> none  [the longest x1 195 us: local(): lax.all_to_all(doubled.reshape(devices * capacity, features), 'expert', s...]
    pallas_call x0 -> x1, Pallas kernels: none -> 129 us  [fused(): pl.pallas_call(functools.partial(fused_kernel, planes, cap, chunks), out_...]
    dot_general x4 -> x0, matrix products: 28.9 us -> none  [the longest x1 12.6 us: swiglu_rows(): both_parts = jnp.dot(inputs, weights, preferred_element_type=jnp.float32)]
    all_to_all x2 -> x0, local copies, waits for them, and re-layouts: 20 us -> none  [the longest x1 12.6 us: local(): lax.all_to_all(doubled.reshape(devices * capacity, features), 'expert', s...]
    broadcast_in_dim x2 -> x0, local copies, waits for them, and re-layouts: 13.4 us -> none  [local(): jnp.broadcast_to(outgoing.reshape(experts, 1, capacity, features), (exper...]
    ppermute x1 -> x0, waiting for transfers between devices: 13.3 us -> none  [partner_2(): return lax.ppermute(block, axis, route)]
    reshape x1 -> x0, local copies, waits for them, and re-layouts: 13.2 us -> none  [local(): pair_total = (summed.astype(jnp.float32) + partner.astype(jnp.float32)).a...]
    all_to_all x2 -> x0, starting transfers between devices: 11.3 us -> none  [the longest x1 7.59 us: local(): lax.all_to_all(doubled.reshape(devices * capacity, features), 'expert', s...]
  transfers between devices with their start and end apart: 3 -> 0, of which waited for: 3 -> 0; matrix products, arithmetic and copies ran while one was open for 2% -> 0% of each run, Pallas kernels for 0% -> 0%
where the time goes in v1:
time: 141 us
  Pallas kernels  129 us (91%)
  local copies, waits for them, and re-layouts  11.8 us (8%)
    pallas_call x1, Pallas kernels, fused(): pl.pallas_call(functools.partial(fused_kernel, planes, cap, chunks), out_...  129 us
    unnamed x4, local copies, waits for them, and re-layouts  11.8 us

profile of v1, /device:TPU:0, one launch (start us, length us, event | category | flops | bytes accessed | tf_op | source)
XLA Modules:
  0.0 141.0 jit_solution(4332064242197845797)
XLA Ops:
  0.0 1.4 copy.7.routes
  1.4 1.4 copy.8.gates
  2.8 7.2 %copy.10 = bf16[1,3584,2,512]{3,1,2,0:T(8,128)(2,1)} copy(bf16[1,3584,2,512]{3,2,1,0:T(2,128)(2,1)} %param.8) | data formatting | bytes 14680064 | tf_op args[3]
  10.0 129.2 %shard_map.55 = bf16[64,3584]{1,0:T(8,128)(2,1)} custom-call(bf16[64,3584]{1,0:T(8,128)(2,1)} %tokens.1, s32[64,8]{1,0:T(8,128)} %copy.7.routes, f32[64,8]{1,0:T(8,128)} %copy.8.gates, bf16[2,3584,512]{2,1,0:T(8,128)(2,1)} %bitcast.6, bf16[512,3584]{1,0:T(8,128)(2,1)} %bitcast.7), custom_call_target="tpu_custom_call" | custom-call | tf_op jit(solution)/shard_map/pallas_call | solution.py:267
  139.2 1.8 %copy.12 = bf16[64,3584]{1,0:T(8,128)(2,1)} copy(bf16[64,3584]{1,0:T(8,128)(2,1)} %shard_map.55) | data formatting | bytes 917504

commit v2 on v1

--- a/solution.py
+++ b/solution.py
@@ -28,7 +28,7 @@
     tokens, routes, gates, gate_up, down,
     out,
     info, line, pack_hot, mix_hi, mix_lo, rows_out, rows_in, acc, hidden,
-    w_up, w_down, y_out, y_in, part, part_own, part_in,
+    w_raw, w_up, w_down, y_out, y_in, part, part_own, part_in,
     i_s, i_r, z_s, z_r, x_s, x_r, y_s, y_r, p_s, p_r, wl, ws, wr, dl, ds, dr,
 ):
     me = lax.axis_index("expert")
@@ -66,10 +66,10 @@
 
     def up_local(j):
         return pltpu.make_async_copy(
-            gate_up.at[:, pl.ds(j * width, width)], w_up.at[0, :, pl.ds(j * width, width)], wl.at[j])
+            gate_up.at[pl.ds(j * width, width)], w_raw.at[pl.ds(j * width, width)], wl.at[j])
 
     def up_swap(j):
-        return remote(gate_up.at[:, pl.ds(j * width, width)],
+        return remote(w_up.at[0, :, pl.ds(j * width, width)],
                       w_up.at[1, :, pl.ds(j * width, width)], ws.at[j], wr.at[j], partner)
 
     down_local = pltpu.make_async_copy(down, w_down.at[pl.ds(0, half)], dl)
@@ -106,10 +106,11 @@
     each_chunk(lambda j: up_local(j).start())
     down_local.start()
 
-    lane = lax.broadcasted_iota(jnp.int32, (tok, 128), 1)
-    weight = jnp.zeros((tok, 128), F32)
-    for k in range(routes.shape[1]):
-        weight = weight + jnp.where(routes[:, k:k + 1] == lane, gates[:, k:k + 1], 0.0)
+    expert_row = lax.broadcasted_iota(jnp.int32, (128, tok), 0)
+    weight_t = jnp.zeros((128, tok), F32)
+    for k in range(routes.shape[0]):
+        weight_t = weight_t + jnp.where(routes[k:k + 1, :] == expert_row, gates[k:k + 1, :], 0.0)
+    weight = jnp.transpose(weight_t)
     member = jnp.where(weight > 0.0, 1.0, 0.0)
     lower = jnp.where(
         lax.broadcasted_iota(jnp.int32, (tok, tok), 1) < lax.broadcasted_iota(jnp.int32, (tok, tok), 0),
@@ -132,7 +133,6 @@
         for d in range(1, planes):
             z_send(d, j).start()
     each_chunk(start_z)
-    each_chunk(lambda j: up_swap(j).start())
     down_swap.start()
 
     def own_line(j):
@@ -174,12 +174,21 @@
         for r in (3, 1, 2):
             x_send(r, j).start()
         rows_in[j, 0:group, :] = packed[0:group]
+
+        up_local(j).wait()
+
+        def split(n, carry):
+            rows = pl.ds(pl.multiple_of(j * width + n * 32, 32), 32)
+            w_up[0, 0, rows, :] = w_raw[rows, 0, :]
+            w_up[0, 1, rows, :] = w_raw[rows, 1, :]
+            return carry
+        lax.fori_loop(0, width // 32, split, 0)
+        up_swap(j).start()
     each_chunk(pack_step)
 
     def up_step(j):
         for r in (1, 2, 3):
             x_send(r, j).wait_recv()
-        up_local(j).wait()
         up_swap(j).wait_recv()
 
         def tile(n, carry):
@@ -259,7 +268,7 @@
     width = features // chunks
     group = planes * cap
     total = planes * tok
-    up = jnp.transpose(gate_up.reshape(features, 2, half), (1, 0, 2))
+    up = gate_up.reshape(features, 2, half)
     down = down_weight.reshape(half, features)
     dma = pltpu.SemaphoreType.DMA
     vmem = pltpu.VMEM
@@ -279,6 +288,7 @@
             vmem((chunks, 4 * group, width), BF16),
             vmem((4, 4 * group, half), F32),
             vmem((4 * group, 2 * half), BF16),
+            vmem((features, 2, half), BF16),
             vmem((2, 2, features, half), BF16),
             vmem((2 * half, features), BF16),
             vmem((chunks, 3 * group, width), BF16),
@@ -292,7 +302,7 @@
         ],
         compiler_params=pltpu.CompilerParams(
             collective_id=0, has_side_effects=True, vmem_limit_bytes=62 * 1024 * 1024),
-    )(tokens, routes, gate_values, up, down)
+    )(tokens, jnp.transpose(routes), jnp.transpose(gate_values), up, down)
 
 
 def partner_2(block, axis, distance):
@@ -329,7 +339,10 @@
     member = (expert_ids[:, None] == jnp.arange(experts, dtype=jnp.int32)[None, :]).astype(
         jnp.int32
     )
-    earlier = jnp.sum((jnp.cumsum(member, axis=0) - member) * member, axis=1)
+    rows = jnp.arange(tok_count * choices, dtype=jnp.int32)
+    before = (rows[None, :] < rows[:, None]).astype(jnp.bfloat16)
+    ranks = jnp.dot(before, member.astype(jnp.bfloat16), preferred_element_type=jnp.float32)
+    earlier = jnp.sum(ranks.astype(jnp.int32) * member, axis=1)
     target = expert_ids * capacity + earlier
     target_hot = (target[:, None] == jnp.arange(targets, dtype=jnp.int32)[None, :]).astype(
         jnp.bfloat16

time: 141 us -> 131 us (0.929)
  local copies, waits for them, and re-layouts: 11.8 us -> 1.82 us
    unnamed x4 -> x1, local copies, waits for them, and re-layouts: 11.8 us -> 1.82 us
where the time goes in v2:
time: 131 us
  Pallas kernels  129 us (98%)
  local copies, waits for them, and re-layouts  1.82 us (1%)
    pallas_call x1, Pallas kernels, fused(): pl.pallas_call(functools.partial(fused_kernel, planes, cap, chunks), out_...  129 us

profile of v2, /device:TPU:0, one launch (start us, length us, event | category | flops | bytes accessed | tf_op | source)
XLA Modules:
  0.0 130.9 jit_solution(1524105590702103327)
XLA Ops:
  0.0 129.1 %shard_map.55 = bf16[64,3584]{1,0:T(8,128)(2,1)} custom-call(bf16[64,3584]{1,0:T(8,128)(2,1)} %tokens.1, s32[8,64]{1,0:T(8,128)} %bitcast.6, f32[8,64]{1,0:T(8,128)} %bitcast.7, bf16[3584,2,512]{2,1,0:T(2,128)(2,1)} %bitcast.4, bf16[512,3584]{1,0:T(8,128)(2,1)} %bitcast.5), custom_call_target="tpu_custom_call" | custom-call | tf_op jit(solution)/shard_map/pallas_call | solution.py:276
  129.1 1.8 %copy.7 = bf16[64,3584]{1,0:T(8,128)(2,1)} copy(bf16[64,3584]{1,0:T(8,128)(2,1)} %shard_map.55) | data formatting | bytes 917504

commit v3 on v2

--- a/solution.py
+++ b/solution.py
@@ -78,9 +78,41 @@
     def info_send(d):
         return remote(info.at[z], info.at[z], i_s.at[d - 1], i_r.at[d - 1], z_peer(d))
 
-    def z_send(d, j):
-        return remote(tokens.at[:, columns(j)], line.at[j, own_rows],
-                      z_s.at[d - 1, j], z_r.at[d - 1, j], z_peer(d))
+    def block_rows(block):
+        return pl.ds(pl.multiple_of(block * tok, 16), tok)
+
+    last = planes - 1
+    sides = ((1, me + 8), (-1, me - 8))
+
+    def z_copy(side, step, j, block):
+        sign, peer = sides[side]
+        k = side * last + step - 1
+        where = line.at[j, block_rows(block)]
+        return remote(where, where, z_s.at[k, j], z_r.at[k, j], peer)
+
+    def inside(block):
+        return jnp.logical_and(block >= 0, block <= last)
+
+    def z_sending(side, step):
+        sign, _ = sides[side]
+        block = z - sign * (step - 1)
+        return jnp.logical_and(inside(block), inside(z + sign)), block
+
+    def z_start(step, j):
+        for side in range(2):
+            allowed, block = z_sending(side, step)
+
+            @pl.when(allowed)
+            def _():
+                z_copy(side, step, j, block).start()
+
+    def z_wait(step, j):
+        for side in range(2):
+            block = z - sides[side][0] * step
+
+            @pl.when(inside(block))
+            def _():
+                z_copy(side, step, j, block).wait_recv()
 
     def x_send(r, j):
         return remote(rows_out.at[j, pl.ds((r - 1) * group, group)],
@@ -129,15 +161,13 @@
     for d in range(1, planes):
         info_send(d).start()
 
-    def start_z(j):
-        for d in range(1, planes):
-            z_send(d, j).start()
-    each_chunk(start_z)
-    down_swap.start()
-
     def own_line(j):
         line[j, own_rows, :] = tokens[:, columns(j)]
     each_chunk(own_line)
+    ahead = min(2, chunks)
+    for j in range(ahead):
+        z_start(1, j)
+    down_swap.start()
 
     for d in range(1, planes):
         info_send(d).wait_recv()
@@ -167,8 +197,6 @@
     mix_lo[...] = (mix - high.astype(F32)).astype(BF16)
 
     def pack_step(j):
-        for d in range(1, planes):
-            z_send(d, j).wait_recv()
         packed = jnp.dot(pack_hot[...], line[j], preferred_element_type=F32).astype(BF16)
         rows_out[j] = packed[group:]
         for r in (3, 1, 2):
@@ -184,7 +212,23 @@
             return carry
         lax.fori_loop(0, width // 32, split, 0)
         up_swap(j).start()
-    each_chunk(pack_step)
+
+    def gather_step(i, carry):
+        @pl.when(i + ahead < chunks)
+        def _():
+            z_start(1, i + ahead)
+        for step in range(1, planes):
+            j = i - (step - 1)
+
+            @pl.when(jnp.logical_and(j >= 0, j < chunks))
+            def _():
+                z_wait(step, j)
+                if step < last:
+                    z_start(step + 1, j)
+                else:
+                    pack_step(j)
+        return carry
+    lax.fori_loop(0, chunks + planes - 2, gather_step, 0)
 
     def up_step(j):
         for r in (1, 2, 3):
@@ -247,7 +291,12 @@
 
     def drain(j):
         for d in range(1, planes):
-            z_send(d, j).wait_send()
+            for side in range(2):
+                allowed, block = z_sending(side, d)
+
+                @pl.when(allowed)
+                def _():
+                    z_copy(side, d, j, block).wait_send()
             p_send(d, j).wait_send()
         for r in (1, 2, 3):
             x_send(r, j).wait_send()
@@ -297,7 +346,7 @@
             vmem((chunks, total, width), F32),
             vmem((chunks, planes - 1, tok, width), BF16),
             dma((planes - 1,)), dma((planes - 1,)),
-            *pairs(planes - 1), *pairs(3), *pairs(3), *pairs(planes - 1),
+            *pairs(2 * (planes - 1)), *pairs(3), *pairs(3), *pairs(planes - 1),
             dma((chunks,)), dma((chunks,)), dma((chunks,)), dma, dma, dma,
         ],
         compiler_params=pltpu.CompilerParams(

time: 131 us -> 126 us (0.962)
  Pallas kernels: 129 us -> 124 us
    pallas_call x1, Pallas kernels: 129 us -> 124 us  [fused(): pl.pallas_call(functools.partial(fused_kernel, planes, cap, chunks), out_...]
where the time goes in v3:
time: 126 us
  Pallas kernels  124 us (98%)
  local copies, waits for them, and re-layouts  1.82 us (1%)
    pallas_call x1, Pallas kernels, fused(): pl.pallas_call(functools.partial(fused_kernel, planes, cap, chunks), out_...  124 us

profile of v3, /device:TPU:0, one launch (start us, length us, event | category | flops | bytes accessed | tf_op | source)
XLA Modules:
  0.0 126.3 jit_solution(2545351110304434570)
XLA Ops:
  0.0 124.5 %shard_map.55 = bf16[64,3584]{1,0:T(8,128)(2,1)} custom-call(bf16[64,3584]{1,0:T(8,128)(2,1)} %tokens.1, s32[8,64]{1,0:T(8,128)} %bitcast.6, f32[8,64]{1,0:T(8,128)} %bitcast.7, bf16[3584,2,512]{2,1,0:T(2,128)(2,1)} %bitcast.4, bf16[512,3584]{1,0:T(8,128)(2,1)} %bitcast.5), custom_call_target="tpu_custom_call" | custom-call | tf_op jit(solution)/shard_map/pallas_call | solution.py:325
  124.5 1.8 %copy.7 = bf16[64,3584]{1,0:T(8,128)(2,1)} copy(bf16[64,3584]{1,0:T(8,128)(2,1)} %shard_map.55) | data formatting | bytes 917504
